TPU v7x, 32 devices: a whole 2x2x4 slice. The times are simulated.
32 devices in a mesh: dom: 8 (over y, x, core), rep: 4 (over z).
Axes of the slice: x: 2, y: 2, z: 4, core: 2. Of those that a mesh axis runs over, the one named last changes fastest.
Arguments:
- features: float32 [2048, 256], P('dom'), may hold values from -6 to 6
- tile_values: bfloat16 [8, 64, 128, 128], P('dom', 'rep'), may hold values from 0 to 0.03125
- tile_rows: int32 [8, 64], P('dom', 'rep'), may hold values from 0 to 1
- tile_cols: int32 [8, 64], P('dom', 'rep'), may hold values from 0 to 15, as said below
- weight: float32 [256, 256], replicated, may hold values from -0.375 to 0.375
- bias: float32 [256], replicated, may hold values from -3 to 3
- cotangent: float32 [2048, 256], P('dom'), may hold values from -6 to 6
Outputs:
- activations: float32 [2048, 256], P('dom')
- grad_features: float32 [2048, 256], P('dom')
- grad_weight: float32 [256, 256], replicated
- grad_bias: float32 [256], replicated
Inputs may be any that keep to these rules, and one draw needn't show every extreme that they name: `tile_cols`: within each share of 16 consecutive tiles of a partition, every tile column 0 to 15 appears exactly once.
All inputs are finite; a program needn't handle non-finite values.
Results may differ from a plain program's by a relative error of at most 0.0003.
Values sent between devices are 32-bit elements; how exact they have to be, the bound alone decides.
A program may use at most 64 MiB of HBM per device.

v0:
```python
import jax
import jax.numpy as jnp
from jax import lax
from jax.sharding import PartitionSpec as P


def body(features, tile_values, tile_rows, tile_cols, weight, bias, cotangent):
    highest = lax.Precision.HIGHEST
    values = tile_values[0].astype(jnp.float32)
    row_ids = tile_rows[0]
    col_ids = tile_cols[0]
    tile_size = values.shape[1]
    node_rows = features.shape[0]
    feat_width = features.shape[1]
    row_blocks = node_rows // tile_size
    shard_piece = lax.all_gather(features, "dom", axis=0, tiled=True)
    block_count = shard_piece.shape[0] // tile_size
    blocks = shard_piece.reshape(block_count, tile_size, feat_width)
    offsets = col_ids[:, None]
    select = (offsets == jnp.arange(block_count, dtype=jnp.int32)[None, :]).astype(jnp.float32)
    selected = jnp.einsum("sn,nif->sif", select, blocks, precision=highest)
    products = jnp.einsum("sij,sjf->sif", values, selected, precision=highest)
    row_select = (row_ids[None, :] == jnp.arange(row_blocks, dtype=jnp.int32)[:, None]).astype(
        jnp.float32
    )
    partial_rows = jnp.einsum("bs,sif->bif", row_select, products, precision=highest).reshape(
        node_rows, feat_width
    )
    aggregated = lax.psum(partial_rows, "rep")
    before = jnp.dot(aggregated, weight, precision=highest) + bias
    gate_value = jax.nn.sigmoid(before)
    output = before * gate_value
    grad_pre = cotangent * gate_value * (1.0 + before * (1.0 - gate_value))
    messages = jnp.dot(grad_pre, weight.T, precision=highest)
    weight_term = jnp.dot(aggregated.T, grad_pre, precision=highest)
    activations, messages, weight_term, bias_term = (
        output,
        messages,
        weight_term,
        jnp.sum(grad_pre, axis=0),
    )
    grad_weight, grad_bias = lax.psum((weight_term, bias_term), "dom")
    message_blocks = messages.reshape(row_blocks, tile_size, feat_width)
    picked_messages = jnp.einsum("bs,bif->sif", row_select, message_blocks, precision=highest)
    returned = jnp.einsum("sji,sjf->sif", values, picked_messages, precision=highest)
    block_count = node_rows * lax.axis_size("dom") // tile_size
    offsets = col_ids[None, :]
    select = (offsets == jnp.arange(block_count, dtype=jnp.int32)[:, None]).astype(jnp.float32)
    source_part = lax.psum_scatter(
        jnp.einsum("ns,sif->nif", select, returned, precision=highest).reshape(
            node_rows * lax.axis_size("dom"), feat_width
        ),
        "dom",
        scatter_dimension=0,
        tiled=True,
    )
    grad_features = lax.psum(source_part, "rep")
    return (activations, grad_features, grad_weight, grad_bias)


def solution(mesh):
    return jax.shard_map(
        body,
        mesh=mesh,
        in_specs=(
            P("dom", None),
            P("dom", "rep", None, None),
            P("dom", "rep"),
            P("dom", "rep"),
            P(),
            P(),
            P("dom", None),
        ),
        out_specs=(P("dom", None), P("dom", None), P(), P()),
        check_vma=False,
    )
```

profile of v0, /device:TPU:0, one launch (start us, length us, event | category | flops | bytes accessed | tf_op | source)
XLA Modules:
  0.0 246.7 jit_solution(1948898299063535947)
XLA Ops:
  7.2 0.7 all-gather.2.cloned.1.call-update
  8.0 32.6 %all-gather.2.cloned.1.call-done = f32[2048,256]{1,0:T(8,128)} async-done(((f32[256,256]{1,0:T(8,128)}), f32[2048,256]{1,0:T(8,128)}) %all-gather.2.cloned.1.call-update) | async-done | bytes 2097168 | tf_op jit(solution)/shard_map/all_gather | solution.py:16
  40.5 3.9 %fusion.8 = f32[16,128,256]{2,0,1:T(8,128)S(1)} fusion(f32[16,128,256]{2,1,0:T(8,128)} %bitcast.35, s32[16]{0:T(128)} %bitcast.40), kind=kOutput, calls=%fused_computation.8 | convolution fusion | flops 100663552 | bytes 4194368 | tf_op jit(solution)/shard_map/sn,nif->sif/dot_general | solution.py:21
  44.5 4.1 %fusion.6 = f32[16,256,128]{2,1,0:T(8,128)} fusion(f32[16,128,256]{2,0,1:T(8,128)S(1)} %fusion.8, bf16[1,16,128,128]{3,2,1,0:T(8,128)(2,1)S(1)} %copy-done), kind=kOutput, calls=%fused_computation.6 | convolution fusion | flops 805306368 | bytes 4718592 | tf_op jit(solution)/shard_map/sij,sjf->sif/dot_general | solution.py:22
  48.5 2.2 copy.15
  50.8 0.8 fusion.2
  51.6 0.7 copy.11
  52.4 0.2 reduce-scatter.2.cloned.1.call-start
  52.6 35.2 %all-reduce.4.cloned.1.call-done = f32[256,256]{1,0:T(8,128)} async-done(((f32[256,256]{1,0:T(8,128)}), f32[256,256]{1,0:T(8,128)}) %all-reduce.4.cloned.1.call-update) | async-done | bytes 262160 | tf_op jit(solution)/shard_map/psum | solution.py:29
  87.9 2.1 fusion.25
  90.0 0.4 fusion.26
  90.4 1.1 fusion.12
  91.5 2.7 %fusion.4 = f32[16,256,128]{2,1,0:T(8,128)S(1)} fusion(f32[16,128,256]{2,0,1:T(8,128)S(1)} %fusion.12, bf16[1,16,128,128]{3,2,1,0:T(8,128)(2,1)S(1)} %copy-done), kind=kOutput, calls=%fused_computation.4 | convolution fusion | flops 805306368 | bytes 4718592 | tf_op jit(solution)/shard_map/sji,sjf->sif/dot_general | solution.py:45
  94.3 2.1 copy.18
  96.4 2.7 %fusion = f32[16,128,256]{2,0,1:T(8,128)S(1)} fusion(f32[16,256,128]{1,0,2:T(8,128)} %copy.18, s32[16]{0:T(128)S(1)} %bitcast.41), kind=kOutput, calls=%fused_computation | convolution fusion | flops 100663552 | bytes 4194368 | tf_op jit(solution)/shard_map/ns,sif->nif/dot_general | solution.py:50
  99.1 2.6 %copy.12 = f32[16,128,256]{2,1,0:T(8,128)} copy(f32[16,128,256]{2,0,1:T(8,128)S(1)} %fusion) | data formatting | bytes 4194304 | tf_op jit(solution)/shard_map/ns,sif->nif/dot_general | solution.py:50
  101.7 0.9 copy-done.2
  102.6 1.3 fusion.27
  103.9 38.8 %reduce-scatter.2.cloned.1.call-done = f32[256,256]{1,0:T(8,128)} async-done(((f32[2048,256]{1,0:T(8,128)}), f32[256,256]{1,0:T(8,128)}) %reduce-scatter.2.cloned.1.call-update) | async-done | bytes 262160 | tf_op jit(solution)/shard_map/reduce_scatter | solution.py:49
  142.8 13.2 %psum.31 = f32[256]{0:T(256)} all-reduce(f32[256]{0:T(256)S(1)} %get-tuple-element.4), channel_id=1, replica_groups=mesh['dom'=8,'rep'=4] {'dom'}, use_global_device_ids=true, to_apply=%region_5.0 | all-reduce | flops 256 | bytes 2048 | tf_op jit(solution)/shard_map/psum | solution.py:42
  156.0 43.8 %all-reduce.8.cloned.1.call-done = f32[256,256]{1,0:T(8,128)} async-done(((f32[256,256]{1,0:T(8,128)}), f32[256,256]{1,0:T(8,128)}) %all-reduce.8.cloned.1.call-update) | async-done | bytes 262160 | tf_op jit(solution)/shard_map/psum | solution.py:42
  199.8 37.0 %all-reduce.6.cloned.1.call-done = f32[256,256]{1,0:T(8,128)} async-done(((f32[256,256]{1,0:T(8,128)}), f32[256,256]{1,0:T(8,128)}) %all-reduce.6.cloned.1.call-update) | async-done | bytes 262160 | tf_op jit(solution)/shard_map/psum | solution.py:57
  236.8 1.7 copy.30
  238.5 1.7 copy.31
  (21 shorter events, 0.3 us)
Async XLA Ops:
  7.2 37.3 %copy-start = (bf16[1,16,128,128]{3,2,1,0:T(8,128)(2,1)S(1)}, bf16[1,16,128,128]{3,2,1,0:T(8,128)(2,1)}, u32[]{:S(2)}) copy-start(bf16[1,16,128,128]{3,2,1,0:T(8,128)(2,1)} %param.8) | copy-start | bytes 1572868
  7.2 33.4 %all-gather.2.cloned.1.call-start = ((), (), s32[]{:S(2)}) async-start(), calls=%async_computation.1 | async-start | bytes 2359296 | tf_op jit(solution)/shard_map/all_gather | solution.py:16
  7.9 79.9 %all-reduce.4.cloned.1.call-start = ((), (), s32[]{:S(2)}) async-start(), calls=%async_computation.2 | async-start | bytes 524288 | tf_op jit(solution)/shard_map/psum | solution.py:29
  48.5 2.3 copy-start.3
  50.8 37.1 %copy-start.1 = (f32[256,256]{1,0:T(8,128)S(1)}, f32[256,256]{1,0:T(8,128)}, u32[]{:S(2)}) copy-start(f32[256,256]{1,0:T(8,128)} %param.11) | copy-start | bytes 786436
  50.8 37.0 %copy-start.5 = (f32[256,256]{1,0:T(8,128)S(1)}, f32[256,256]{1,0:T(8,128)}, u32[]{:S(2)}) copy-start(f32[256,256]{1,0:T(8,128)} %param.13) | copy-start | bytes 786436
  50.8 37.0 %copy-start.6 = (f32[256]{0:T(256)S(1)}, f32[256]{0:T(256)}, u32[]{:S(2)}) copy-start(f32[256]{0:T(256)} %param.12) | copy-start | bytes 3076
  52.4 90.4 %reduce-scatter.2.cloned.1.call-start = ((), (), s32[]{:S(2)}) async-start(), calls=%async_computation.3 | async-start | bytes 2359296 | tf_op jit(solution)/shard_map/reduce_scatter | solution.py:49
  94.3 2.1 copy-start.4
  101.6 0.9 copy-start.2
  101.6 98.2 %all-reduce.8.cloned.1.call-start = ((), (), s32[]{:S(2)}) async-start(), calls=%async_computation.5 | async-start | bytes 524288 | tf_op jit(solution)/shard_map/psum | solution.py:42
  103.9 132.9 %all-reduce.6.cloned.1.call-start = ((), (), s32[]{:S(2)}) async-start(), calls=%async_computation.4 | async-start | bytes 524288 | tf_op jit(solution)/shard_map/psum | solution.py:57
Sparse Core Ops, SparseCore 0:
  9.9 30.5 all-gather.1
  52.5 35.2 all-reduce.3
  101.8 40.9 reduce-scatter.1
  146.2 53.5 all-reduce.7
  202.1 34.6 all-reduce.5
where the time goes:
time: 247 us
  waiting for transfers between devices  188 us (76%)
  matrix products  19.2 us (8%)
  between operations  13.9 us (6%)
  blocking collectives  13.2 us (5%)
  local copies, waits for them, and re-layouts  11.8 us (5%)
    psum x1, waiting for transfers between devices, body(): grad_weight, grad_bias = lax.psum((weight_term, bias_term), 'dom')  43.8 us
    reduce_scatter x1, waiting for transfers between devices, body(): lax.psum_scatter(jnp.einsum('ns,sif->nif', select, returned, precision=hi...  38.8 us
    psum x1, waiting for transfers between devices, body(): grad_features = lax.psum(source_part, 'rep')  37 us
    psum x1, waiting for transfers between devices, body(): aggregated = lax.psum(partial_rows, 'rep')  35.2 us
    all_gather x1, waiting for transfers between devices, body(): shard_piece = lax.all_gather(features, 'dom', axis=0, tiled=True)  32.6 us
    psum x1, blocking collectives, body(): grad_weight, grad_bias = lax.psum((weight_term, bias_term), 'dom')  13.2 us
  transfers between devices with their start and end apart: 5, of which 5 were waited for; matrix products, arithmetic and copies ran while one was open for 1% of the time, Pallas kernels for 0%

commit v1 on v0

--- a/solution.py
+++ b/solution.py
@@ -13,7 +13,14 @@
     node_rows = features.shape[0]
     feat_width = features.shape[1]
     row_blocks = node_rows // tile_size
-    shard_piece = lax.all_gather(features, "dom", axis=0, tiled=True)
+    size = lax.axis_size("dom")
+    hops = [(i, (i + 1) % size) for i in range(size)]
+    pieces = [features]
+    for far in range(1, size):
+        pieces = [lax.ppermute(pieces[0], "dom", hops), *pieces]
+    full = jnp.concatenate(pieces, axis=0)
+    shift = (lax.axis_index("dom") + 1) * pieces[-1].shape[0]
+    shard_piece = jnp.roll(full, shift, axis=0)
     block_count = shard_piece.shape[0] // tile_size
     blocks = shard_piece.reshape(block_count, tile_size, feat_width)
     offsets = col_ids[:, None]

time: 247 us -> 263 us (1.065)
  waiting for transfers between devices: 188 us -> 204 us
    ppermute x0 -> x7, waiting for transfers between devices: none -> 47.3 us  [body(): pieces = [lax.ppermute(pieces[0], 'dom', hops), *pieces]]
    all_gather x1 -> x0, waiting for transfers between devices: 32.6 us -> none  [body(): shard_piece = lax.all_gather(features, 'dom', axis=0, tiled=True)]
  transfers between devices with their start and end apart: 5 -> 11, of which waited for: 5 -> 11; matrix products, arithmetic and copies ran while one was open for 1% -> 0% of each run, Pallas kernels for 0% -> 0%
where the time goes in v1:
time: 263 us
  waiting for transfers between devices  204 us (78%)
  matrix products  17.6 us (7%)
  between operations  14 us (5%)
  blocking collectives  13.2 us (5%)
  local copies, waits for them, and re-layouts  12.7 us (5%)
    ppermute x7, waiting for transfers between devices, body(): pieces = [lax.ppermute(pieces[0], 'dom', hops), *pieces]  47.3 us
    psum x1, waiting for transfers between devices, body(): grad_weight, grad_bias = lax.psum((weight_term, bias_term), 'dom')  43.9 us
    reduce_scatter x1, waiting for transfers between devices, body(): lax.psum_scatter(jnp.einsum('ns,sif->nif', select, returned, precision=hi...  39.7 us
    psum x1, waiting for transfers between devices, body(): grad_features = lax.psum(source_part, 'rep')  37 us
    psum x1, waiting for transfers between devices, body(): aggregated = lax.psum(partial_rows, 'rep')  36.3 us
    psum x1, blocking collectives, body(): grad_weight, grad_bias = lax.psum((weight_term, bias_term), 'dom')  13.2 us
  transfers between devices with their start and end apart: 11, of which 11 were waited for; matrix products, arithmetic and copies ran while one was open for 0% of the time, Pallas kernels for 0%

profile of v1, /device:TPU:0, one launch (start us, length us, event | category | flops | bytes accessed | tf_op | source)
XLA Modules:
  0.0 262.7 jit_solution(15597217092499227991)
XLA Ops:
  7.7 7.2 %collective-permute-done = f32[256,256]{1,0:T(8,128)S(1)} collective-permute-done((f32[256,256]{1,0:T(8,128)}, f32[256,256]{1,0:T(8,128)S(1)}, u32[]{:S(2)}, u32[]{:S(2)}) %collective-permute-start) | collective-permute-done | bytes 262176 | tf_op jit(solution)/shard_map/ppermute | solution.py:20
  14.9 6.7 %collective-permute-done.1 = f32[256,256]{1,0:T(8,128)S(1)} collective-permute-done((f32[256,256]{1,0:T(8,128)S(1)}, f32[256,256]{1,0:T(8,128)S(1)}, u32[]{:S(2)}, u32[]{:S(2)}) %collective-permute-start.1) | collective-permute-done | bytes 262176 | tf_op jit(solution)/shard_map/ppermute | solution.py:20
  21.6 6.7 %collective-permute-done.2 = f32[256,256]{1,0:T(8,128)S(1)} collective-permute-done((f32[256,256]{1,0:T(8,128)S(1)}, f32[256,256]{1,0:T(8,128)S(1)}, u32[]{:S(2)}, u32[]{:S(2)}) %collective-permute-start.2) | collective-permute-done | bytes 262176 | tf_op jit(solution)/shard_map/ppermute | solution.py:20
  28.3 6.7 %collective-permute-done.3 = f32[256,256]{1,0:T(8,128)S(1)} collective-permute-done((f32[256,256]{1,0:T(8,128)S(1)}, f32[256,256]{1,0:T(8,128)S(1)}, u32[]{:S(2)}, u32[]{:S(2)}) %collective-permute-start.3) | collective-permute-done | bytes 262176 | tf_op jit(solution)/shard_map/ppermute | solution.py:20
  35.0 6.7 %collective-permute-done.4 = f32[256,256]{1,0:T(8,128)S(1)} collective-permute-done((f32[256,256]{1,0:T(8,128)S(1)}, f32[256,256]{1,0:T(8,128)S(1)}, u32[]{:S(2)}, u32[]{:S(2)}) %collective-permute-start.4) | collective-permute-done | bytes 262176 | tf_op jit(solution)/shard_map/ppermute | solution.py:20
  41.7 6.7 %collective-permute-done.5 = f32[256,256]{1,0:T(8,128)S(1)} collective-permute-done((f32[256,256]{1,0:T(8,128)S(1)}, f32[256,256]{1,0:T(8,128)S(1)}, u32[]{:S(2)}, u32[]{:S(2)}) %collective-permute-start.5) | collective-permute-done | bytes 262176 | tf_op jit(solution)/shard_map/ppermute | solution.py:20
  48.4 6.7 %collective-permute-done.6 = f32[256,256]{1,0:T(8,128)S(1)} collective-permute-done((f32[256,256]{1,0:T(8,128)S(1)}, f32[256,256]{1,0:T(8,128)S(1)}, u32[]{:S(2)}, u32[]{:S(2)}) %collective-permute-start.6) | collective-permute-done | bytes 262176 | tf_op jit(solution)/shard_map/ppermute | solution.py:20
  56.9 2.3 fusion.8
  59.2 4.1 %fusion.6 = f32[16,256,128]{2,1,0:T(8,128)} fusion(f32[16,128,256]{2,0,1:T(8,128)S(1)} %fusion.8, bf16[1,16,128,128]{3,2,1,0:T(8,128)(2,1)S(1)} %copy-done), kind=kOutput, calls=%fused_computation.6 | convolution fusion | flops 805306368 | bytes 4718592 | tf_op jit(solution)/shard_map/sij,sjf->sif/dot_general | solution.py:29
  63.3 2.3 copy.15
  67.4 36.3 %all-reduce.4.cloned.1.call-done = f32[256,256]{1,0:T(8,128)} async-done(((f32[256,256]{1,0:T(8,128)}), f32[256,256]{1,0:T(8,128)}) %all-reduce.4.cloned.1.call-update) | async-done | bytes 262160 | tf_op jit(solution)/shard_map/psum | solution.py:36
  103.7 2.1 fusion.25
  106.3 1.1 fusion.12
  107.4 2.7 %fusion.4 = f32[16,256,128]{2,1,0:T(8,128)S(1)} fusion(f32[16,128,256]{2,0,1:T(8,128)S(1)} %fusion.12, bf16[1,16,128,128]{3,2,1,0:T(8,128)(2,1)S(1)} %copy-done), kind=kOutput, calls=%fused_computation.4 | convolution fusion | flops 805306368 | bytes 4718592 | tf_op jit(solution)/shard_map/sji,sjf->sif/dot_general | solution.py:52
  110.1 2.1 copy.18
  112.2 2.7 %fusion = f32[16,128,256]{2,0,1:T(8,128)S(1)} fusion(f32[16,256,128]{1,0,2:T(8,128)} %copy.18, s32[16]{0:T(128)S(1)} %bitcast.41), kind=kOutput, calls=%fused_computation | convolution fusion | flops 100663552 | bytes 4194368 | tf_op jit(solution)/shard_map/ns,sif->nif/dot_general | solution.py:57
  114.9 2.6 copy.12
  117.5 1.3 fusion.27
  118.9 39.7 %reduce-scatter.2.cloned.1.call-done = f32[256,256]{1,0:T(8,128)} async-done(((f32[2048,256]{1,0:T(8,128)}), f32[256,256]{1,0:T(8,128)}) %reduce-scatter.2.cloned.1.call-update) | async-done | bytes 262160 | tf_op jit(solution)/shard_map/reduce_scatter | solution.py:56
  158.6 13.2 %psum.31 = f32[256]{0:T(256)} all-reduce(f32[256]{0:T(256)S(1)} %get-tuple-element.4), channel_id=1, replica_groups=mesh['dom'=8,'rep'=4] {'dom'}, use_global_device_ids=true, to_apply=%region_5.6 | all-reduce | flops 256 | bytes 2048 | tf_op jit(solution)/shard_map/psum | solution.py:49
  171.9 43.9 %all-reduce.8.cloned.1.call-done = f32[256,256]{1,0:T(8,128)} async-done(((f32[256,256]{1,0:T(8,128)}), f32[256,256]{1,0:T(8,128)}) %all-reduce.8.cloned.1.call-update) | async-done | bytes 262160 | tf_op jit(solution)/shard_map/psum | solution.py:49
  215.8 37.0 %all-reduce.6.cloned.1.call-done = f32[256,256]{1,0:T(8,128)} async-done(((f32[256,256]{1,0:T(8,128)}), f32[256,256]{1,0:T(8,128)}) %all-reduce.6.cloned.1.call-update) | async-done | bytes 262160 | tf_op jit(solution)/shard_map/psum | solution.py:64
  252.8 1.7 copy.45
  254.5 1.7 copy.46
  (51 shorter events, 4.6 us)
Async XLA Ops:
  7.2 52.1 %copy-start = (bf16[1,16,128,128]{3,2,1,0:T(8,128)(2,1)S(1)}, bf16[1,16,128,128]{3,2,1,0:T(8,128)(2,1)}, u32[]{:S(2)}) copy-start(bf16[1,16,128,128]{3,2,1,0:T(8,128)(2,1)} %param.8) | copy-start | bytes 1572868
  7.2 49.3 %copy-start.1 = (f32[256,256]{1,0:T(8,128)S(1)}, f32[256,256]{1,0:T(8,128)}, u32[]{:S(2)}) copy-start(f32[256,256]{1,0:T(8,128)} %param.7) | copy-start | bytes 786436
  7.2 96.5 %all-reduce.4.cloned.1.call-start = ((), (), s32[]{:S(2)}) async-start(), calls=%async_computation.1 | async-start | bytes 524288 | tf_op jit(solution)/shard_map/psum | solution.py:36
  7.2 7.7 %collective-permute-start = (f32[256,256]{1,0:T(8,128)}, f32[256,256]{1,0:T(8,128)S(1)}, u32[]{:S(2)}, u32[]{:S(2)}) collective-permute-start(f32[256,256]{1,0:T(8,128)} %param.7), channel_id=1, source_target_pairs={{0,4},{4,8},{8,12},{12,16},{16,20},{20,24},{24,28},{28,0},{1,5},{5... | collective-permute-start | bytes 786440 | tf_op jit(solution)/shard_map/ppermute | solution.py:20
  14.9 6.7 %collective-permute-start.1 = (f32[256,256]{1,0:T(8,128)S(1)}, f32[256,256]{1,0:T(8,128)S(1)}, u32[]{:S(2)}, u32[]{:S(2)}) collective-permute-start(f32[256,256]{1,0:T(8,128)S(1)} %collective-permute-done), channel_id=1, source_target_pairs={{0,4},{4,8},{8,12},{12,16},{16,20},{20,24},{24,28},{28,0},{1,5},{5... | collective-permute-start | bytes 786440 | tf_op jit(solution)/shard_map/ppermute | solution.py:20
  21.6 6.7 %collective-permute-start.2 = (f32[256,256]{1,0:T(8,128)S(1)}, f32[256,256]{1,0:T(8,128)S(1)}, u32[]{:S(2)}, u32[]{:S(2)}) collective-permute-start(f32[256,256]{1,0:T(8,128)S(1)} %collective-permute-done.1), channel_id=1, source_target_pairs={{0,4},{4,8},{8,12},{12,16},{16,20},{20,24},{24,28},{28,0},{1,5},{5... | collective-permute-start | bytes 786440 | tf_op jit(solution)/shard_map/ppermute | solution.py:20
  28.3 6.7 %collective-permute-start.3 = (f32[256,256]{1,0:T(8,128)S(1)}, f32[256,256]{1,0:T(8,128)S(1)}, u32[]{:S(2)}, u32[]{:S(2)}) collective-permute-start(f32[256,256]{1,0:T(8,128)S(1)} %collective-permute-done.2), channel_id=1, source_target_pairs={{0,4},{4,8},{8,12},{12,16},{16,20},{20,24},{24,28},{28,0},{1,5},{5... | collective-permute-start | bytes 786440 | tf_op jit(solution)/shard_map/ppermute | solution.py:20
  35.0 6.7 %collective-permute-start.4 = (f32[256,256]{1,0:T(8,128)S(1)}, f32[256,256]{1,0:T(8,128)S(1)}, u32[]{:S(2)}, u32[]{:S(2)}) collective-permute-start(f32[256,256]{1,0:T(8,128)S(1)} %collective-permute-done.3), channel_id=1, source_target_pairs={{0,4},{4,8},{8,12},{12,16},{16,20},{20,24},{24,28},{28,0},{1,5},{5... | collective-permute-start | bytes 786440 | tf_op jit(solution)/shard_map/ppermute | solution.py:20
  41.7 6.7 %collective-permute-start.5 = (f32[256,256]{1,0:T(8,128)S(1)}, f32[256,256]{1,0:T(8,128)S(1)}, u32[]{:S(2)}, u32[]{:S(2)}) collective-permute-start(f32[256,256]{1,0:T(8,128)S(1)} %collective-permute-done.4), channel_id=1, source_target_pairs={{0,4},{4,8},{8,12},{12,16},{16,20},{20,24},{24,28},{28,0},{1,5},{5... | collective-permute-start | bytes 786440 | tf_op jit(solution)/shard_map/ppermute | solution.py:20
  48.4 6.7 %collective-permute-start.6 = (f32[256,256]{1,0:T(8,128)S(1)}, f32[256,256]{1,0:T(8,128)S(1)}, u32[]{:S(2)}, u32[]{:S(2)}) collective-permute-start(f32[256,256]{1,0:T(8,128)S(1)} %collective-permute-done.5), channel_id=1, source_target_pairs={{0,4},{4,8},{8,12},{12,16},{16,20},{20,24},{24,28},{28,0},{1,5},{5... | collective-permute-start | bytes 786440 | tf_op jit(solution)/shard_map/ppermute | solution.py:20
  56.2 0.7 copy-start.5
  59.2 6.4 %copy-start.4 = (s32[1,16]{1,0:T(1,128)S(1)}, s32[1,16]{1,0:T(1,128)}, u32[]{:S(2)}) copy-start(s32[1,16]{1,0:T(1,128)} %param.9) | copy-start | bytes 196
  63.3 40.4 %copy-start.2 = (f32[256,256]{1,0:T(8,128)S(1)}, f32[256,256]{1,0:T(8,128)}, u32[]{:S(2)}) copy-start(f32[256,256]{1,0:T(8,128)} %param.11) | copy-start | bytes 786436
  63.3 40.4 %copy-start.6 = (f32[256,256]{1,0:T(8,128)S(1)}, f32[256,256]{1,0:T(8,128)}, u32[]{:S(2)}) copy-start(f32[256,256]{1,0:T(8,128)} %param.13) | copy-start | bytes 786436
  63.3 40.4 %copy-start.7 = (f32[256]{0:T(256)S(1)}, f32[256]{0:T(256)}, u32[]{:S(2)}) copy-start(f32[256]{0:T(256)} %param.12) | copy-start | bytes 3076
  67.2 91.5 %reduce-scatter.2.cloned.1.call-start = ((), (), s32[]{:S(2)}) async-start(), calls=%async_computation.2 | async-start | bytes 2359296 | tf_op jit(solution)/shard_map/reduce_scatter | solution.py:56
  114.9 2.6 %copy-start.3 = (f32[256,256]{1,0:T(8,128)S(1)}, f32[256,256]{1,0:T(8,128)}, u32[]{:S(2)}) copy-start(f32[256,256]{1,0:T(8,128)} %all-reduce.4.cloned.1.call-done) | copy-start | bytes 786436
  117.5 98.3 %all-reduce.8.cloned.1.call-start = ((), (), s32[]{:S(2)}) async-start(), calls=%async_computation.4 | async-start | bytes 524288 | tf_op jit(solution)/shard_map/psum | solution.py:49
  118.9 133.9 %all-reduce.6.cloned.1.call-start = ((), (), s32[]{:S(2)}) async-start(), calls=%async_computation.3 | async-start | bytes 524288 | tf_op jit(solution)/shard_map/psum | solution.py:64
Sparse Core Ops, SparseCore 0:
  67.3 36.3 all-reduce.3
  117.6 40.9 reduce-scatter.1
  162.2 53.5 all-reduce.7
  218.1 34.6 all-reduce.5
